TPU v7x, 32 devices: a whole 2x2x4 slice. The times are simulated.
32 devices in a mesh: gx: 8 (over z, core), gy: 4 (over y, x).
Axes of the slice: x: 2, y: 2, z: 4, core: 2. Of those that a mesh axis runs over, the one named last changes fastest.
Arguments:
- snapshots: float32 [128, 64, 16, 128], P(None, 'gx', 'gy'), may hold values from -700 to 700
- viscosity: float32 [64, 16, 128], P('gx', 'gy'), may hold values from 0.2 to 1
- velocity: float32 [3, 64, 16, 128], P(None, 'gx', 'gy'), may hold values from -4 to 4
Outputs:
- modes: bfloat16 [128, 64, 16, 128], P(None, 'gx', 'gy')
- factor: float32 [128, 128], replicated
All inputs are finite; a program needn't handle non-finite values.
Results may differ from a plain program's by a relative error of at most 0.001.
Values sent between devices are 32-bit elements; how exact they have to be, the bound alone decides.
A program may use at most 64 MiB of HBM per device.

v0:
```python
import jax
import jax.numpy as jnp
from jax import lax
from jax.sharding import PartitionSpec as P


def extended(x, sides, width):
    for axis, dim in sides:
        peers, length = (lax.axis_size(axis), x.shape[dim])
        up = [(i, (i + 1) % peers) for i in range(peers - 1)]
        down = [(j, i) for i, j in up]
        last = lax.slice_in_dim(x, length - width, length, axis=dim)
        initial = lax.slice_in_dim(x, 0, width, axis=dim)
        before = lax.ppermute(last, axis, up)
        after = lax.ppermute(initial, axis, down)
        x = jnp.concatenate([before, x, after], axis=dim)
    return x


def unit_shift(direction, offset):
    shifts = [0, 0, 0]
    shifts[direction] = offset
    return shifts


def take_cells(padded, shifts, sizes):
    return padded[
        ...,
        2 + shifts[0] : 2 + shifts[0] + sizes[0],
        2 + shifts[1] : 2 + shifts[1] + sizes[1],
        2 + shifts[2] : 2 + shifts[2] + sizes[2],
    ]


def stencil(field_pad, visc_pad, velocity):
    sizes = velocity.shape[1:]
    center = take_cells(field_pad, [0, 0, 0], sizes)
    visc_mid = take_cells(visc_pad, [0, 0, 0], sizes)
    total = jnp.zeros(center.shape, jnp.float32)
    for direction in range(3):
        plus_one = take_cells(field_pad, unit_shift(direction, 1), sizes)
        minus_one = take_cells(field_pad, unit_shift(direction, -1), sizes)
        plus_two = take_cells(field_pad, unit_shift(direction, 2), sizes)
        minus_two = take_cells(field_pad, unit_shift(direction, -2), sizes)
        slope = (8.0 * (plus_one - minus_one) - (plus_two - minus_two)) / 12.0
        visc_plus = 0.5 * (visc_mid + take_cells(visc_pad, unit_shift(direction, 1), sizes))
        visc_minus = 0.5 * (visc_mid + take_cells(visc_pad, unit_shift(direction, -1), sizes))
        spread = visc_plus * (plus_one - center) - visc_minus * (center - minus_one)
        total = total + velocity[direction] * slope - spread
    return total


def lower_factor(gram):
    order = gram.shape[0]
    positions = jnp.arange(order, dtype=jnp.int32)

    def column_step(column, lower):
        row_here = lax.dynamic_slice_in_dim(lower, column, 1, 0)[0]
        gram_col = lax.dynamic_slice_in_dim(gram, column, 1, 1)[:, 0]
        reduced = gram_col - jnp.dot(
            lower, row_here, precision=lax.Precision.HIGHEST, preferred_element_type=jnp.float32
        )
        pivot = jnp.sum(jnp.where(positions == column, reduced, 0.0))
        root = jnp.sqrt(pivot)
        fresh = jnp.where(
            positions > column, reduced / root, jnp.where(positions == column, root, 0.0)
        )
        return lax.dynamic_update_slice_in_dim(lower, fresh[:, None], column, 1)

    return lax.fori_loop(0, order, column_step, jnp.zeros(gram.shape, jnp.float32))


def lower_inverse(lower):
    order = lower.shape[0]
    positions = jnp.arange(order, dtype=jnp.int32)

    def row_step(row, inverse):
        lower_row = lax.dynamic_slice_in_dim(lower, row, 1, 0)[0]
        pivot = jnp.sum(jnp.where(positions == row, lower_row, 0.0))
        below = jnp.where(positions < row, lower_row, 0.0)
        unit_row = jnp.where(positions == row, 1.0, 0.0).astype(jnp.float32)
        fresh = (
            unit_row
            - jnp.dot(
                below, inverse, precision=lax.Precision.HIGHEST, preferred_element_type=jnp.float32
            )
        ) / pivot
        return lax.dynamic_update_slice_in_dim(inverse, fresh[None, :], row, 0)

    return lax.fori_loop(0, order, row_step, jnp.zeros(lower.shape, jnp.float32))


def upper_factor(gram):
    return lower_factor(gram).T


def per_device(snapshots, viscosity, velocity):
    count_snaps = snapshots.shape[0]
    stacked = jnp.concatenate([snapshots, viscosity[None]], axis=0)
    padded = extended(stacked, (("gx", 1), ("gy", 2)), 2)
    padded = jnp.pad(padded, ((0, 0), (0, 0), (0, 0), (2, 2)))
    field_pad = padded[:count_snaps]
    visc_pad = padded[count_snaps]
    resid = stencil(field_pad, visc_pad, velocity)
    local_cells = resid.shape[1] * resid.shape[2] * resid.shape[3]
    count_cells = local_cells * lax.axis_size("gx") * lax.axis_size("gy")
    matrix = resid.reshape(count_snaps, local_cells)
    local_gram = jnp.dot(
        matrix, matrix.T, precision=lax.Precision.HIGHEST, preferred_element_type=jnp.float32
    ) / float(count_cells)
    factor = upper_factor(lax.psum(local_gram, ("gx", "gy")))
    inverse = lower_inverse(factor.T)
    solved = jnp.dot(
        inverse, matrix, precision=lax.Precision.HIGHEST, preferred_element_type=jnp.float32
    )
    modes = solved.reshape(resid.shape).astype(jnp.bfloat16)
    return (modes, factor)


def solution(mesh):
    placed = (P(None, "gx", "gy", None), P("gx", "gy", None), P(None, "gx", "gy", None))
    return jax.shard_map(
        per_device,
        mesh=mesh,
        in_specs=placed,
        out_specs=(P(None, "gx", "gy", None), P()),
        check_vma=False,
    )
```

profile of v0, /device:TPU:0, one launch (start us, length us, event | category | flops | bytes accessed | tf_op | source)
XLA Modules:
  0.0 738.5 jit_solution(123663377305363070)
XLA Ops:
  7.2 1.7 pad_maximum_fusion.12
  8.9 1.3 collective-permute-start
  10.2 3.1 collective-permute-start.1
  13.3 1.5 collective-permute-done.1
  14.8 1.5 pad_maximum_fusion
  16.3 1.2 fusion.46
  17.8 5.1 collective-permute-start.2
  23.3 1.5 collective-permute-start.3
  24.8 2.1 pad_maximum_fusion.1
  26.9 37.4 %collective-permute-done.2 = f32[129,12,2,128]{3,1,2,0:T(8,128)S(1)} collective-permute-done((f32[129,12,2,128]{3,1,2,0:T(8,128)S(1)}, f32[129,12,2,128]{3,1,2,0:T(8,128)S(1)}, u32[]{:S(2)}, u32[]{:S(2)}) %collective-permute-start.2) | collective-permute-done | bytes 1585184 | tf_op jit(solution)/shard_map/ppermute | solution.py:14
  65.1 46.4 %collective-permute-done.3 = f32[129,12,2,128]{3,1,2,0:T(8,128)S(1)} collective-permute-done((f32[129,12,2,128]{3,1,2,0:T(8,128)S(1)}, f32[129,12,2,128]{3,1,2,0:T(8,128)S(1)}, u32[]{:S(2)}, u32[]{:S(2)}) %collective-permute-start.3) | collective-permute-done | bytes 1585184 | tf_op jit(solution)/shard_map/ppermute | solution.py:15
  112.3 18.5 %select_maximum_fusion = f32[129,12,8,132]{3,2,1,0:T(8,128)S(1)} fusion(f32[129,12,2,128]{3,2,1,0:T(2,128)S(1)} %copy.54, f32[129,12,2,128]{3,2,1,0:T(2,128)S(1)} %copy.53, f32[129,2,4,128]{3,2,1,0:T(4,128)S(1)} %collective-permute-done, f32[129,2,4,128]{3,2,1,0:T(4,128)S(1)} %collective-permute-done.1, f32[1,8,4,128]{3,2,1,0:T(4,128)S(1)} %bitcast.88, ...), kind=kLoop, calls=%fused_computation.28 | loop fusion | flops 22885632 | bytes 12879360 | tf_op jit(solution)/shard_map/concatenate | solution.py:16
  131.0 13.3 %fusion.24 = f32[128,8,4,128]{3,2,1,0:T(4,128)} fusion(f32[129,12,8,132]{3,2,1,0:T(8,128)S(1)} %select_maximum_fusion, f32[129,12,2,128]{3,2,1,0:T(2,128)S(1)} %copy.53, f32[129,2,4,128]{3,2,1,0:T(4,128)S(1)} %collective-permute-done, f32[129,2,4,128]{3,2,1,0:T(4,128)S(1)} %collective-permute-done.1, f32[1,8,4,128]{3,2,1,0:T(4,128)S(1)} %bitcast.89, ...), kind=kLoop, calls=%fused_computation.41 | loop fusion | flops 26738688 | bytes 25362432 | tf_op jit(solution)/shard_map/sub | solution.py:49
  144.3 2.0 copy.60
  146.3 4.1 fusion.38
  150.4 126.7 %all-reduce.3.cloned.1.call-done = f32[128,128]{1,0:T(8,128)} async-done(((f32[128,128]{1,0:T(8,128)}), f32[128,128]{1,0:T(8,128)}) %all-reduce.3.cloned.1.call-update) | async-done | bytes 65552 | tf_op jit(solution)/shard_map/psum | solution.py:111
  277.2 0.9 copy.59
  278.1 259.0 %while.30 = (s32[]{:T(128)}, f32[128,128]{1,0:T(8,128)S(1)}, f32[128,128]{0,1:T(8,128)S(1)}, s32[]{:T(128)}, s32[]{:T(128)}) while((s32[]{:T(128)}, f32[128,128]{1,0:T(8,128)S(1)}, f32[128,128]{0,1:T(8,128)S(1)}, s32[]{:T(128)}, s32[]{:T(128)}) %tuple.88), condition=%wide.region_3.4_spmd.clone.clone, body=%wide.region_1.3_spmd.clone.clone.sunk | while | flops 197761 | bytes 71765 | solution.py:70
  278.4 0.8 fusion.59
  280.3 0.8 fusion.59
  282.3 0.8 fusion.59
  284.3 0.8 fusion.59
  286.3 0.8 fusion.59
  288.4 0.8 fusion.59
  290.4 0.8 fusion.59
  292.4 0.8 fusion.59
  294.4 0.8 fusion.59
  296.5 0.8 fusion.59
  298.5 0.8 fusion.59
  300.5 0.8 fusion.59
  302.5 0.8 fusion.59
  304.5 0.8 fusion.59
  306.6 0.8 fusion.59
  308.6 0.8 fusion.59
  310.6 0.8 fusion.59
  312.6 0.8 fusion.59
  314.6 0.8 fusion.59
  316.7 0.8 fusion.59
  318.7 0.8 fusion.59
  320.7 0.8 fusion.59
  322.7 0.8 fusion.59
  324.8 0.8 fusion.59
  326.8 0.8 fusion.59
  328.8 0.8 fusion.59
  330.8 0.8 fusion.59
  537.8 190.1 %while.31 = (s32[]{:T(128)}, f32[128,128]{1,0:T(8,128)S(1)}, f32[128,128]{1,0:T(8,128)S(1)}, s32[]{:T(128)}, s32[]{:T(128)}) while((s32[]{:T(128)}, f32[128,128]{1,0:T(8,128)S(1)}, f32[128,128]{1,0:T(8,128)S(1)}, s32[]{:T(128)}, s32[]{:T(128)}) %tuple.91), condition=%wide.region_6.7_spmd.clone.clone, body=%wide.region_4.6_spmd.clone.clone.sunk | while | flops 197761 | bytes 71237 | solution.py:90
  727.9 1.9 fusion.35
  729.9 1.8 copy.62
  (888 shorter events, 334.6 us)
Async XLA Ops:
  7.2 7.6 %copy-start.1 = (f32[8,4,128]{2,1,0:T(4,128)S(1)}, f32[8,4,128]{2,1,0:T(4,128)}, u32[]{:S(2)}) copy-start(f32[8,4,128]{2,1,0:T(4,128)} %param.8) | copy-start | bytes 49156
  7.2 7.6 %copy-start = (f32[128,8,4,128]{3,2,1,0:T(4,128)S(1)}, f32[128,8,4,128]{3,2,1,0:T(4,128)}, u32[]{:S(2)}) copy-start(f32[128,8,4,128]{3,2,1,0:T(4,128)} %param.7) | copy-start | bytes 6291460
  7.2 270.0 %all-reduce.3.cloned.1.call-start = ((), (), s32[]{:S(2)}) async-start(), calls=%async_computation | async-start | bytes 131072 | tf_op jit(solution)/shard_map/psum | solution.py:111
  8.9 4.4 collective-permute-start
  10.2 4.6 collective-permute-start.1
  17.8 6.9 copy-start.2
  17.8 46.4 %collective-permute-start.2 = (f32[129,12,2,128]{3,1,2,0:T(8,128)S(1)}, f32[129,12,2,128]{3,1,2,0:T(8,128)S(1)}, u32[]{:S(2)}, u32[]{:S(2)}) collective-permute-start(f32[129,12,2,128]{3,1,2,0:T(8,128)S(1)} %copy.51), channel_id=1, source_target_pairs={{0,1},{1,2},{2,3},{4,5},{5,6},{6,7},{8,9},{9,10},{10,11},{12,13},{... | collective-permute-start | bytes 4755464 | tf_op jit(solution)/shard_map/ppermute | solution.py:14
  23.3 88.2 %collective-permute-start.3 = (f32[129,12,2,128]{3,1,2,0:T(8,128)S(1)}, f32[129,12,2,128]{3,1,2,0:T(8,128)S(1)}, u32[]{:S(2)}, u32[]{:S(2)}) collective-permute-start(f32[129,12,2,128]{3,1,2,0:T(8,128)S(1)} %copy.52), channel_id=1, source_target_pairs={{1,0},{2,1},{3,2},{5,4},{6,5},{7,6},{9,8},{10,9},{11,10},{13,12},{... | collective-permute-start | bytes 4755464 | tf_op jit(solution)/shard_map/ppermute | solution.py:15
Sparse Core Ops, SparseCore 0:
  150.5 126.5 all-reduce.2
where the time goes:
time: 742 us; the launch traced here: 738 us
  waiting for transfers between devices  212 us (29%)
  matrix products  210 us (28%)
  other arithmetic  122 us (16%)
  loops' own time  95.5 us (13%)
  local copies, waits for them, and re-layouts  73.3 us (10%)
  between operations  14.2 us (2%)
  starting transfers between devices  11 us (1%)
    psum x1, waiting for transfers between devices, per_device(): factor = upper_factor(lax.psum(local_gram, ('gx', 'gy')))  127 us
    dot_general x128, matrix products, column_step(): jnp.dot(lower, row_here, precision=lax.Precision.HIGHEST, preferred_eleme...  105 us
    dot_general x128, matrix products, row_step(): jnp.dot(below, inverse, precision=lax.Precision.HIGHEST, preferred_elemen...  99.4 us
    another operation x1, loops' own time, lower_factor(): lax.fori_loop(0, order, column_step, jnp.zeros(gram.shape, jnp.float32))  92.9 us
    reduce_sum x128, other arithmetic, row_step(): pivot = jnp.sum(jnp.where(positions == row, lower_row, 0.0))  84.1 us
    ppermute x2, waiting for transfers between devices, extended(): after = lax.ppermute(initial, axis, down)  46.4 us
    dynamic_update_slice x128, local copies, waits for them, and re-layouts, column_step(): return lax.dynamic_update_slice_in_dim(lower, fresh[:, None], column, 1)  45.8 us
    ppermute x2, waiting for transfers between devices, extended(): before = lax.ppermute(last, axis, up)  38.8 us
  transfers between devices with their start and end apart: 5, of which 4 were waited for; matrix products, arithmetic and copies ran while one was open for 0% of the time, Pallas kernels for 0%

commit v1 on v0

v1 whole, which is shorter than its diff:
```python
import functools

import jax
import jax.numpy as jnp
from jax import lax
from jax.experimental import pallas as pl
from jax.experimental.pallas import tpu as pltpu
from jax.sharding import PartitionSpec as P

MESH = pl.DeviceIdType.MESH
HIGH = lax.Precision.HIGHEST


def dot(a, b, transposed=False):
    return lax.dot_general(
        a, b, (((1,), (1 if transposed else 0,)), ((), ())),
        precision=HIGH, preferred_element_type=jnp.float32,
    )


def kernel(
    dims, peers, chunk, cells_total,
    snap_ref, visc_ref, vel_ref, modes_ref, factor_ref,
    wide, near_visc, pad_visc, coef, resid, rows_out, part_y, part_x, inv, low, diag,
    send_halo, recv_halo, send_visc, recv_visc, send_y, recv_y, send_x, recv_x,
):
    snaps, nx, ny, nz = dims
    gx_n, gy_n = peers
    cells = nx * ny
    chunks = snaps // chunk
    gx, gy = lax.axis_index("gx"), lax.axis_index("gy")

    def along_y(other):
        return {"gx": gx, "gy": other}

    def along_x(other):
        return {"gx": other, "gy": gy}

    barrier = pltpu.get_barrier_semaphore()
    for off in range(1, gy_n):
        pl.semaphore_signal(barrier, inc=1, device_id=along_y(lax.rem(gy + off, gy_n)), device_id_type=MESH)
    for off in range(1, gx_n):
        pl.semaphore_signal(barrier, inc=1, device_id=along_x(lax.rem(gx + off, gx_n)), device_id_type=MESH)

    def spread(p):
        def plane(i, carry):
            for j in range(ny):
                wide[p, i + 2, j + 2] = snap_ref[
                    pl.ds(p * chunk * cells + i * ny + j, chunk, stride=cells), :
                ]
            return carry

        lax.fori_loop(0, nx, plane, 0)

    def halo_copies(p):
        mid_x, mid_y = pl.ds(2, nx), pl.ds(2, ny)
        table = (
            (gy < gy_n - 1, along_y(gy + 1), (mid_x, pl.ds(ny, 2)), (mid_x, pl.ds(0, 2))),
            (gy > 0, along_y(gy - 1), (mid_x, pl.ds(2, 2)), (mid_x, pl.ds(ny + 2, 2))),
            (gx < gx_n - 1, along_x(gx + 1), (pl.ds(nx, 2), mid_y), (pl.ds(0, 2), mid_y)),
            (gx > 0, along_x(gx - 1), (pl.ds(2, 2), mid_y), (pl.ds(nx + 2, 2), mid_y)),
        )
        return [
            (
                there,
                pltpu.make_async_remote_copy(
                    src_ref=wide.at[p, src[0], src[1]],
                    dst_ref=wide.at[p, dst[0], dst[1]],
                    send_sem=send_halo.at[p, way],
                    recv_sem=recv_halo.at[p, way],
                    device_id=who,
                    device_id_type=MESH,
                ),
            )
            for way, (there, who, src, dst) in enumerate(table)
        ]

    def visc_copies():
        table = (
            (gy < gy_n - 1, along_y(gy + 1)),
            (gy > 0, along_y(gy - 1)),
            (gx < gx_n - 1, along_x(gx + 1)),
            (gx > 0, along_x(gx - 1)),
        )
        return [
            (
                there,
                pltpu.make_async_remote_copy(
                    src_ref=visc_ref,
                    dst_ref=near_visc.at[way],
                    send_sem=send_visc.at[way],
                    recv_sem=recv_visc.at[way],
                    device_id=who,
                    device_id_type=MESH,
                ),
            )
            for way, (there, who) in enumerate(table)
        ]

    arrives = (gy > 0, gy < gy_n - 1, gx > 0, gx < gx_n - 1)

    def start(copies):
        for there, copy in copies:
            pl.when(there)(copy.start)

    def wait_recv(copies):
        for way, (_, copy) in enumerate(copies):
            pl.when(arrives[way])(copy.wait_recv)

    def wait_send(copies):
        for there, copy in copies:
            pl.when(there)(copy.wait_send)

    spread(0)
    pl.semaphore_wait(barrier, gx_n + gy_n - 2)
    start(visc_copies())
    start(halo_copies(0))
    for p in range(1, chunks):
        spread(p)
        start(halo_copies(p))

    def border(way):
        rows_y = jnp.zeros((chunks, nx, 2, chunk, nz), jnp.float32)
        rows_x = jnp.zeros((chunks, 2, ny, chunk, nz), jnp.float32)
        if way == 0:
            wide[:, 2:nx + 2, 0:2] = rows_y
        elif way == 1:
            wide[:, 2:nx + 2, ny + 2:ny + 4] = rows_y
        elif way == 2:
            wide[:, 0:2, 2:ny + 2] = rows_x
        else:
            wide[:, nx + 2:nx + 4, 2:ny + 2] = rows_x

    for way in range(4):
        pl.when(jnp.logical_not(arrives[way]))(functools.partial(border, way))

    inv[...] = jnp.zeros_like(inv)
    pad_visc[...] = jnp.zeros_like(pad_visc)
    pad_visc[1:nx + 1, 1:ny + 1, :] = visc_ref[...]
    wait_recv(visc_copies())

    def visc_border(way):
        if way == 0:
            pad_visc[1:nx + 1, 0:1, :] = near_visc[0, :, ny - 1:ny, :]
        elif way == 1:
            pad_visc[1:nx + 1, ny + 1:ny + 2, :] = near_visc[1, :, 0:1, :]
        elif way == 2:
            pad_visc[0:1, 1:ny + 1, :] = near_visc[2, nx - 1:nx, :, :]
        else:
            pad_visc[nx + 1:nx + 2, 1:ny + 1, :] = near_visc[3, 0:1, :, :]

    for way in range(4):
        pl.when(arrives[way])(functools.partial(visc_border, way))

    lane3 = lax.broadcasted_iota(jnp.int32, (nx, ny, nz), 2)
    mid = pad_visc[1:nx + 1, 1:ny + 1, :]
    around = (
        (pad_visc[2:nx + 2, 1:ny + 1, :], pad_visc[0:nx, 1:ny + 1, :]),
        (pad_visc[1:nx + 1, 2:ny + 2, :], pad_visc[1:nx + 1, 0:ny, :]),
        (
            jnp.where(lane3 < nz - 1, pltpu.roll(mid, nz - 1, 2), 0.0),
            jnp.where(lane3 > 0, pltpu.roll(mid, 1, 2), 0.0),
        ),
    )
    for d in range(3):
        coef[d, 0] = vel_ref[d] * (8.0 / 12.0)
        coef[d, 1] = vel_ref[d] * (1.0 / 12.0)
        coef[d, 2] = 0.5 * (mid + around[d][0])
        coef[d, 3] = 0.5 * (mid + around[d][1])

    lane = lax.broadcasted_iota(jnp.int32, (chunk, nz), 1)

    def stencil(p):
        def plane(i, carry):
            for j in range(ny):
                c = wide[p, i + 2, j + 2]
                near = (
                    (wide[p, i + 3, j + 2], wide[p, i + 1, j + 2], wide[p, i + 4, j + 2], wide[p, i, j + 2]),
                    (wide[p, i + 2, j + 3], wide[p, i + 2, j + 1], wide[p, i + 2, j + 4], wide[p, i + 2, j]),
                    (
                        jnp.where(lane < nz - 1, pltpu.roll(c, nz - 1, 1), 0.0),
                        jnp.where(lane > 0, pltpu.roll(c, 1, 1), 0.0),
                        jnp.where(lane < nz - 2, pltpu.roll(c, nz - 2, 1), 0.0),
                        jnp.where(lane > 1, pltpu.roll(c, 2, 1), 0.0),
                    ),
                )
                total = None
                for d in range(3):
                    up, down, up2, down2 = near[d]
                    w8, w1, vp, vm = (coef[d, t, i, pl.ds(j, 1), :] for t in range(4))
                    term = (w8 * (up - down) - w1 * (up2 - down2)) - (vp * (up - c) - vm * (c - down))
                    total = term if total is None else total + term
                resid[pl.ds(p * chunk, chunk), pl.ds(pl.multiple_of((i * ny + j) * nz, nz), nz)] = total
            return carry

        lax.fori_loop(0, nx, plane, 0)

    def sum_copies(p, axis):
        me, count, who, part, send, recv = (
            (gy, gy_n, along_y, part_y, send_y, recv_y) if axis == "gy" else (gx, gx_n, along_x, part_x, send_x, recv_x)
        )
        out, into = [], []
        for off in range(1, count):
            to, frm = lax.rem(me + off, count), lax.rem(me + count - off, count)
            for list_, slot, k in ((out, me, to), (into, frm, frm)):
                list_.append(
                    pltpu.make_async_remote_copy(
                        src_ref=part.at[p, slot], dst_ref=part.at[p, slot],
                        send_sem=send.at[p, off], recv_sem=recv.at[p, off],
                        device_id=who(k), device_id_type=MESH,
                    )
                )
        return out, into

    def added(part, p, count):
        total = part[p, 0]
        for k in range(1, count):
            total = total + part[p, k]
        return total

    def gram(p):
        top = (p + 1) * chunk
        panel = dot(resid[p * chunk:top, :], resid[0:top, :], transposed=True) * (1.0 / cells_total)
        if top < snaps:
            panel = jnp.concatenate([panel, jnp.zeros((chunk, snaps - top), jnp.float32)], axis=1)
        part_y[p, gy] = panel
        for copy in sum_copies(p, "gy")[0]:
            copy.start()

    def gram_x(p):
        for copy in sum_copies(p, "gy")[1]:
            copy.wait_recv()
        part_x[p, gx] = added(part_y, p, gy_n)
        for copy in sum_copies(p, "gx")[0]:
            copy.start()

    row_s = lax.broadcasted_iota(jnp.int32, (chunk, snaps), 0)
    lane_s = lax.broadcasted_iota(jnp.int32, (chunk, snaps), 1)

    def padded(x):
        return x if chunk == snaps else jnp.concatenate([x, jnp.zeros((snaps - chunk, snaps), jnp.float32)], axis=0)

    def factor(p):
        for copy in sum_copies(p, "gx")[1]:
            copy.wait_recv()
        g = added(part_x, p, gx_n)
        w0 = p * chunk
        here = pl.ds(w0, chunk)
        if p > 0:
            off = dot(g, inv[...], transposed=True)
            g = pltpu.roll(g, snaps - w0, 1) - dot(off, padded(off), transposed=True)
            back = dot(off, inv[...])
            low[here, :] = off
        else:
            low[here, :] = jnp.zeros((chunk, snaps), jnp.float32)
        a = jnp.where(lane_s < chunk, g, jnp.where(lane_s == row_s + chunk, 1.0, 0.0))
        for k in range(chunk):
            scaled = a[k:k + 1, :] / a[k:k + 1, k:k + 1]
            a = a - jnp.where(row_s > k, a[:, k:k + 1], 0.0) * scaled
        pivots = jnp.sum(jnp.where(lane_s == row_s, a, 0.0), axis=1, keepdims=True)
        a = a / jnp.sqrt(pivots)
        upper = jnp.where((lane_s >= row_s) & (lane_s < chunk), a, 0.0)
        own = jnp.where(lane_s < chunk, pltpu.roll(a, snaps - chunk, 1), 0.0)
        if p > 0:
            diag[here, :] = pltpu.roll(upper, w0, 1)
            inv[here, :] = pltpu.roll(own, w0, 1) - dot(own, padded(back))
        else:
            diag[here, :] = upper
            inv[here, :] = own

    def modes(p):
        top = (p + 1) * chunk
        weights = inv[p * chunk:top, 0:top]

        def plane(i, carry):
            first = pl.multiple_of(i * ny * nz, ny * nz)
            block = dot(weights, resid[0:top, pl.ds(first, ny * nz)])
            for j in range(ny):
                rows_out[pl.ds(i * ny + j, chunk, stride=cells), :] = block[:, j * nz:(j + 1) * nz]
            return carry

        lax.fori_loop(0, nx, plane, 0)
        modes_ref[p * chunk * cells:top * cells, :] = rows_out[...].astype(jnp.bfloat16)

    for p in range(chunks):
        wait_recv(halo_copies(p))
        stencil(p)
        gram(p)
        if p > 0:
            factor(p - 1)
            modes(p - 1)
        gram_x(p)
    factor(chunks - 1)
    modes(chunks - 1)
    factor_ref[...] = low[...].T + diag[...]

    wait_send(visc_copies())
    for p in range(chunks):
        wait_send(halo_copies(p))
        for axis in ("gy", "gx"):
            for copy in sum_copies(p, axis)[0]:
                copy.wait_send()


def per_device(gx_n, gy_n, snapshots, viscosity, velocity):
    snaps, nx, ny, nz = snapshots.shape
    cells = nx * ny
    chunk = snaps // 4
    chunks = snaps // chunk
    f32 = jnp.float32
    dma = pltpu.SemaphoreType.DMA
    vmem = pl.BlockSpec(memory_space=pltpu.VMEM)
    modes, factor = pl.pallas_call(
        functools.partial(
            kernel, (snaps, nx, ny, nz), (gx_n, gy_n), chunk, float(cells * nz * gx_n * gy_n)
        ),
        out_shape=(
            jax.ShapeDtypeStruct((snaps * cells, nz), jnp.bfloat16),
            jax.ShapeDtypeStruct((snaps, snaps), f32),
        ),
        in_specs=[vmem] * 3,
        out_specs=(vmem, vmem),
        scratch_shapes=[
            pltpu.VMEM((chunks, nx + 4, ny + 4, chunk, nz), f32),
            pltpu.VMEM((4, nx, ny, nz), f32),
            pltpu.VMEM((nx + 2, ny + 2, nz), f32),
            pltpu.VMEM((3, 4, nx, ny, nz), f32),
            pltpu.VMEM((snaps, cells * nz), f32),
            pltpu.VMEM((chunk * cells, nz), f32),
            pltpu.VMEM((chunks, gy_n, chunk, snaps), f32),
            pltpu.VMEM((chunks, gx_n, chunk, snaps), f32),
            pltpu.VMEM((snaps, snaps), f32),
            pltpu.VMEM((snaps, snaps), f32),
            pltpu.VMEM((snaps, snaps), f32),
            dma((chunks, 4)), dma((chunks, 4)), dma((4,)), dma((4,)),
            dma((chunks, gy_n)), dma((chunks, gy_n)), dma((chunks, gx_n)), dma((chunks, gx_n)),
        ],
        compiler_params=pltpu.CompilerParams(
            collective_id=0, has_side_effects=True, vmem_limit_bytes=48 * 1024 * 1024
        ),
        name="pod",
    )(snapshots.reshape(snaps * cells, nz), viscosity, velocity)
    return modes.reshape(snaps, nx, ny, nz), factor


def solution(mesh):
    placed = (P(None, "gx", "gy", None), P("gx", "gy", None), P(None, "gx", "gy", None))
    return jax.shard_map(
        functools.partial(per_device, mesh.shape["gx"], mesh.shape["gy"]),
        mesh=mesh,
        in_specs=placed,
        out_specs=(P(None, "gx", "gy", None), P()),
        check_vma=False,
    )
```

time: 742 us -> 99.3 us (0.13)
  waiting for transfers between devices: 212 us -> 0 us
  matrix products: 210 us -> 0 us
  other arithmetic: 122 us -> 0 us
  loops' own time: 95.5 us -> 0 us
  Pallas kernels: 0 us -> 93.7 us
  local copies, waits for them, and re-layouts: 73.3 us -> 4.7 us
  between operations: 14.2 us -> 0.65 us
  starting transfers between devices: 11 us -> 0 us
    dot_general x258 -> x0, matrix products: 210 us -> none  [the longest x128 105 us: column_step(): jnp.dot(lower, row_here, precision=lax.Precision.HIGHEST, preferred_eleme...]
    psum x1 -> x0, waiting for transfers between devices: 127 us -> none  [per_device(): factor = upper_factor(lax.psum(local_gram, ('gx', 'gy')))]
    another operation x2 -> x0, loops' own time: 95.5 us -> none  [the longest x1 92.9 us: lower_factor(): lax.fori_loop(0, order, column_step, jnp.zeros(gram.shape, jnp.float32))]
    pallas_call x0 -> x1, Pallas kernels: none -> 93.7 us  [per_device(): pl.pallas_call(functools.partial(kernel, (snaps, nx, ny, nz), (gx_n, gy_n...]
    ppermute x4 -> x0, waiting for transfers between devices: 85.3 us -> none  [the longest x2 46.4 us: extended(): after = lax.ppermute(initial, axis, down)]
    reduce_sum x128 -> x0, other arithmetic: 84.1 us -> none  [row_step(): pivot = jnp.sum(jnp.where(positions == row, lower_row, 0.0))]
    dynamic_update_slice x256 -> x0, local copies, waits for them, and re-layouts: 49.8 us -> none  [the longest x128 45.8 us: column_step(): return lax.dynamic_update_slice_in_dim(lower, fresh[:, None], column, 1)]
    concatenate x4 -> x0, other arithmetic: 23.8 us -> none  [the longest x3 22.2 us: extended(): x = jnp.concatenate([before, x, after], axis=dim)]
  transfers between devices with their start and end apart: 5 -> 0, of which waited for: 4 -> 0; matrix products, arithmetic and copies ran while one was open for 0% -> 0% of each run, Pallas kernels for 0% -> 0%
where the time goes in v1:
time: 99.3 us; the launch traced here: 99 us
  Pallas kernels  93.7 us (94%)
  local copies, waits for them, and re-layouts  4.7 us (5%)
    pallas_call x1, Pallas kernels, per_device(): pl.pallas_call(functools.partial(kernel, (snaps, nx, ny, nz), (gx_n, gy_n...  93.7 us
    unnamed x8, local copies, waits for them, and re-layouts  4.7 us

profile of v1, /device:TPU:0, one launch (start us, length us, event | category | flops | bytes accessed | tf_op | source)
XLA Modules:
  0.0 99.0 jit_solution(8383296632568171618)
XLA Ops:
  0.6 0.0 copy-start
  0.6 1.6 %copy-done = f32[128,8,4,128]{3,2,1,0:T(4,128)S(1)} copy-done((f32[128,8,4,128]{3,2,1,0:T(4,128)S(1)}, f32[128,8,4,128]{3,2,1,0:T(4,128)}, u32[]{:S(2)}) %copy-start) | copy-done | bytes 2097176
  2.2 0.0 copy-start.1
  2.2 0.8 copy-done.1
  3.0 0.0 copy-start.2
  3.0 0.7 copy-done.2
  3.7 93.7 %pod.1 = (bf16[4096,128]{1,0:T(8,128)(2,1)S(1)}, f32[128,128]{1,0:T(8,128)S(1)}) custom-call(f32[4096,128]{1,0:T(8,128)S(1)} %bitcast.2, f32[8,4,128]{2,1,0:T(4,128)S(1)} %copy-done.2, f32[3,8,4,128]{3,2,1,0:T(4,128)S(1)} %copy-done.1), custom_call_target="tpu_custom_call" | custom-call | tf_op jit(solution)/shard_map/pod/pallas_call | solution.py:313
  97.4 1.0 copy.7
  98.4 0.6 copy.8
Async XLA Ops:
  0.6 1.6 %copy-start = (f32[128,8,4,128]{3,2,1,0:T(4,128)S(1)}, f32[128,8,4,128]{3,2,1,0:T(4,128)}, u32[]{:S(2)}) copy-start(f32[128,8,4,128]{3,2,1,0:T(4,128)} %param.3) | copy-start | bytes 6291460
  2.2 0.8 copy-start.1
  3.0 0.7 copy-start.2

commit v2 on v1

--- a/solution.py
+++ b/solution.py
@@ -18,11 +18,17 @@
     )
 
 
+def narrow_dot(a, b, transposed=False):
+    return lax.dot_general(
+        a, b, (((1,), (1 if transposed else 0,)), ((), ())), preferred_element_type=jnp.float32
+    )
+
+
 def kernel(
     dims, peers, chunk, cells_total,
     snap_ref, visc_ref, vel_ref, modes_ref, factor_ref,
-    wide, near_visc, pad_visc, coef, resid, rows_out, part_y, part_x, inv, low, diag,
-    send_halo, recv_halo, send_visc, recv_visc, send_y, recv_y, send_x, recv_x,
+    wide, passing, near_visc, pad_visc, coef, high, rest, rows_out, part_y, part_x, inv, low, diag,
+    send_halo, recv_halo, send_mid, recv_pass, send_pass, recv_mid, send_visc, recv_visc, send_y, recv_y, send_x, recv_x,
 ):
     snaps, nx, ny, nz = dims
     gx_n, gy_n = peers
@@ -52,11 +58,87 @@
 
         lax.fori_loop(0, nx, plane, 0)
 
+    relayed = gy_n == 4
+    if relayed:
+        up_direct, down_direct = (gy == 0) | (gy == 2), (gy == 1) | (gy == 3)
+        from_below, from_above = down_direct, up_direct
+    else:
+        up_direct, down_direct = gy < gy_n - 1, gy > 0
+        from_below, from_above = gy > 0, gy < gy_n - 1
+    half = nx // 2
+    halves = (pl.ds(2, half), pl.ds(2 + half, half))
+    mids = ((1, ny, 0, 0, (0, 3)), (2, 2, ny + 2, 1, (3, 0)))
+
+    def first_hop(p, slot, h):
+        _, row, _, _, relays = mids[slot]
+        return pltpu.make_async_remote_copy(
+            src_ref=wide.at[p, halves[h], pl.ds(row, 2)], dst_ref=passing.at[p, slot],
+            send_sem=send_mid.at[p, int(h)], recv_sem=recv_pass.at[p, slot],
+            device_id=along_y(relays[h]), device_id_type=MESH,
+        )
+
+    def first_hops(p, me):
+        return [first_hop(p, me - 1, h) for h in (1, 0)]
+
+    def second_hop(p, slot, relay):
+        source, _, row, _, relays = mids[slot]
+        h = relays.index(relay)
+        return pltpu.make_async_remote_copy(
+            src_ref=passing.at[p, slot], dst_ref=wide.at[p, halves[h], pl.ds(row, 2)],
+            send_sem=send_pass.at[p, slot], recv_sem=recv_mid.at[p, h],
+            device_id=along_y(3 - source), device_id_type=MESH,
+        )
+
+    def when_at(me, body):
+        pl.when(gy == me)(body)
+
+    def start_first(p):
+        if relayed:
+            for me in (1, 2):
+                def go(me=me):
+                    for copy in first_hops(p, me):
+                        copy.start()
+                when_at(me, go)
+
+    def pass_on(p, late):
+        if relayed:
+            for relay in (0, 3):
+                def go(relay=relay):
+                    slot = (relay == 3) ^ (not late)
+                    copy = second_hop(p, int(slot), relay)
+                    first_hop(p, int(slot), mids[slot][4].index(relay)).wait_recv()
+                    copy.start()
+                when_at(relay, go)
+
+    def wait_mid(p):
+        if relayed:
+            for me in (1, 2):
+                def go(me=me):
+                    for relay in mids[2 - me][4]:
+                        second_hop(p, 2 - me, relay).wait_recv()
+                when_at(me, go)
+
+    def wait_mid_sent(p):
+        if relayed:
+            for me in (1, 2):
+                def go(me=me):
+                    for copy in first_hops(p, me):
+                        copy.wait_send()
+                when_at(me, go)
+
+    def wait_passed(p):
+        if relayed:
+            for relay in (0, 3):
+                def go(relay=relay):
+                    for slot in range(2):
+                        second_hop(p, slot, relay).wait_send()
+                when_at(relay, go)
+
     def halo_copies(p):
         mid_x, mid_y = pl.ds(2, nx), pl.ds(2, ny)
         table = (
-            (gy < gy_n - 1, along_y(gy + 1), (mid_x, pl.ds(ny, 2)), (mid_x, pl.ds(0, 2))),
-            (gy > 0, along_y(gy - 1), (mid_x, pl.ds(2, 2)), (mid_x, pl.ds(ny + 2, 2))),
+            (up_direct, along_y(gy + 1), (mid_x, pl.ds(ny, 2)), (mid_x, pl.ds(0, 2))),
+            (down_direct, along_y(gy - 1), (mid_x, pl.ds(2, 2)), (mid_x, pl.ds(ny + 2, 2))),
             (gx < gx_n - 1, along_x(gx + 1), (pl.ds(nx, 2), mid_y), (pl.ds(0, 2), mid_y)),
             (gx > 0, along_x(gx - 1), (pl.ds(2, 2), mid_y), (pl.ds(nx + 2, 2), mid_y)),
         )
@@ -98,14 +180,15 @@
         ]
 
     arrives = (gy > 0, gy < gy_n - 1, gx > 0, gx < gx_n - 1)
+    arrives_direct = (from_below, from_above) + arrives[2:]
 
     def start(copies):
         for there, copy in copies:
             pl.when(there)(copy.start)
 
-    def wait_recv(copies):
+    def wait_recv(copies, comes):
         for way, (_, copy) in enumerate(copies):
-            pl.when(arrives[way])(copy.wait_recv)
+            pl.when(comes[way])(copy.wait_recv)
 
     def wait_send(copies):
         for there, copy in copies:
@@ -114,10 +197,16 @@
     spread(0)
     pl.semaphore_wait(barrier, gx_n + gy_n - 2)
     start(visc_copies())
-    start(halo_copies(0))
+
+    def send_chunk(p):
+        start_first(p)
+        start(halo_copies(p))
+
+    send_chunk(0)
     for p in range(1, chunks):
         spread(p)
-        start(halo_copies(p))
+        if p == 1:
+            send_chunk(1)
 
     def border(way):
         rows_y = jnp.zeros((chunks, nx, 2, chunk, nz), jnp.float32)
@@ -137,7 +226,7 @@
     inv[...] = jnp.zeros_like(inv)
     pad_visc[...] = jnp.zeros_like(pad_visc)
     pad_visc[1:nx + 1, 1:ny + 1, :] = visc_ref[...]
-    wait_recv(visc_copies())
+    wait_recv(visc_copies(), arrives)
 
     def visc_border(way):
         if way == 0:
@@ -190,7 +279,10 @@
                     w8, w1, vp, vm = (coef[d, t, i, pl.ds(j, 1), :] for t in range(4))
                     term = (w8 * (up - down) - w1 * (up2 - down2)) - (vp * (up - c) - vm * (c - down))
                     total = term if total is None else total + term
-                resid[pl.ds(p * chunk, chunk), pl.ds(pl.multiple_of((i * ny + j) * nz, nz), nz)] = total
+                lanes = pl.ds(pl.multiple_of((i * ny + j) * nz, nz), nz)
+                upper = total.astype(jnp.bfloat16)
+                high[pl.ds(p * chunk, chunk), lanes] = upper
+                rest[pl.ds(p * chunk, chunk), lanes] = (total - upper.astype(jnp.float32)).astype(jnp.bfloat16)
             return carry
 
         lax.fori_loop(0, nx, plane, 0)
@@ -218,9 +310,14 @@
             total = total + part[p, k]
         return total
 
+    def halves_sum(with_high, with_rest):
+        return with_high[:chunk] + (with_high[chunk:] + (with_rest[:chunk] + with_rest[chunk:]))
+
     def gram(p):
         top = (p + 1) * chunk
-        panel = dot(resid[p * chunk:top, :], resid[0:top, :], transposed=True) * (1.0 / cells_total)
+        both = jnp.concatenate([high[p * chunk:top, :], rest[p * chunk:top, :]], axis=0)
+        panel = halves_sum(narrow_dot(both, high[0:top, :], True), narrow_dot(both, rest[0:top, :], True))
+        panel = panel * (1.0 / cells_total)
         if top < snaps:
             panel = jnp.concatenate([panel, jnp.zeros((chunk, snaps - top), jnp.float32)], axis=1)
         part_y[p, gy] = panel
@@ -254,9 +351,20 @@
         else:
             low[here, :] = jnp.zeros((chunk, snaps), jnp.float32)
         a = jnp.where(lane_s < chunk, g, jnp.where(lane_s == row_s + chunk, 1.0, 0.0))
-        for k in range(chunk):
-            scaled = a[k:k + 1, :] / a[k:k + 1, k:k + 1]
-            a = a - jnp.where(row_s > k, a[:, k:k + 1], 0.0) * scaled
+        step = 8
+        for first in range(0, chunk, step):
+            columns = [jnp.broadcast_to(a[:, first + t:first + t + 1], a.shape) for t in range(step)]
+            rows = [a[first + t:first + t + 1, :] for t in range(step)]
+            for t in range(step):
+                k = first + t
+                col = columns[t]
+                over = 1.0 / col[k:k + 1, :]
+                scaled = rows[t] * over
+                a = a - jnp.where(row_s > k, col, 0.0) * scaled
+                for u in range(t + 1, step):
+                    entry = col[first + u:first + u + 1, :]
+                    columns[u] = columns[u] - col * (entry * over)
+                    rows[u] = rows[u] - entry * scaled
         pivots = jnp.sum(jnp.where(lane_s == row_s, a, 0.0), axis=1, keepdims=True)
         a = a / jnp.sqrt(pivots)
         upper = jnp.where((lane_s >= row_s) & (lane_s < chunk), a, 0.0)
@@ -270,11 +378,14 @@
 
     def modes(p):
         top = (p + 1) * chunk
-        weights = inv[p * chunk:top, 0:top]
+        full = inv[p * chunk:top, 0:top]
+        upper = full.astype(jnp.bfloat16)
+        weights = jnp.concatenate([upper, (full - upper.astype(jnp.float32)).astype(jnp.bfloat16)], axis=0)
 
         def plane(i, carry):
             first = pl.multiple_of(i * ny * nz, ny * nz)
-            block = dot(weights, resid[0:top, pl.ds(first, ny * nz)])
+            lanes = pl.ds(first, ny * nz)
+            block = halves_sum(narrow_dot(weights, high[0:top, lanes]), narrow_dot(weights, rest[0:top, lanes]))
             for j in range(ny):
                 rows_out[pl.ds(i * ny + j, chunk, stride=cells), :] = block[:, j * nz:(j + 1) * nz]
             return carry
@@ -283,20 +394,37 @@
         modes_ref[p * chunk * cells:top * cells, :] = rows_out[...].astype(jnp.bfloat16)
 
     for p in range(chunks):
-        wait_recv(halo_copies(p))
+        if p == 0:
+            pass_on(0, False)
+            pass_on(0, True)
+            pass_on(1, False)
+        wait_recv(halo_copies(p), arrives_direct)
+        wait_mid(p)
+        if p + 2 < chunks:
+            wait_send(halo_copies(p))
+            wait_mid_sent(p)
+            send_chunk(p + 2)
         stencil(p)
         gram(p)
+        if p + 1 < chunks:
+            pass_on(p + 1, True)
         if p > 0:
             factor(p - 1)
+        gram_x(p)
+        if p + 2 < chunks:
+            pass_on(p + 2, False)
+        if p > 0:
             modes(p - 1)
-        gram_x(p)
     factor(chunks - 1)
     modes(chunks - 1)
     factor_ref[...] = low[...].T + diag[...]
 
     wait_send(visc_copies())
     for p in range(chunks):
-        wait_send(halo_copies(p))
+        if p + 2 >= chunks:
+            wait_send(halo_copies(p))
+            wait_mid_sent(p)
+        wait_passed(p)
         for axis in ("gy", "gx"):
             for copy in sum_copies(p, axis)[0]:
                 copy.wait_send()
@@ -322,17 +450,20 @@
         out_specs=(vmem, vmem),
         scratch_shapes=[
             pltpu.VMEM((chunks, nx + 4, ny + 4, chunk, nz), f32),
+            pltpu.VMEM((chunks, 2, nx // 2, 2, chunk, nz), f32),
             pltpu.VMEM((4, nx, ny, nz), f32),
             pltpu.VMEM((nx + 2, ny + 2, nz), f32),
             pltpu.VMEM((3, 4, nx, ny, nz), f32),
-            pltpu.VMEM((snaps, cells * nz), f32),
+            pltpu.VMEM((snaps, cells * nz), jnp.bfloat16),
+            pltpu.VMEM((snaps, cells * nz), jnp.bfloat16),
             pltpu.VMEM((chunk * cells, nz), f32),
             pltpu.VMEM((chunks, gy_n, chunk, snaps), f32),
             pltpu.VMEM((chunks, gx_n, chunk, snaps), f32),
             pltpu.VMEM((snaps, snaps), f32),
             pltpu.VMEM((snaps, snaps), f32),
             pltpu.VMEM((snaps, snaps), f32),
-            dma((chunks, 4)), dma((chunks, 4)), dma((4,)), dma((4,)),
+            dma((chunks, 4)), dma((chunks, 4)), dma((chunks, 2)), dma((chunks, 2)), dma((chunks, 2)), dma((chunks, 2)),
+            dma((4,)), dma((4,)),
             dma((chunks, gy_n)), dma((chunks, gy_n)), dma((chunks, gx_n)), dma((chunks, gx_n)),
         ],
         compiler_params=pltpu.CompilerParams(

time: 99.3 us -> 72.6 us (0.73)
  Pallas kernels: 93.7 us -> 67 us
    pallas_call x1, Pallas kernels: 93.7 us -> 67 us  [per_device(): pl.pallas_call(functools.partial(kernel, (snaps, nx, ny, nz), (gx_n, gy_n...]
where the time goes in v2:
time: 72.6 us; the launch traced here: 72.3 us
  Pallas kernels  67 us (92%)
  local copies, waits for them, and re-layouts  4.7 us (6%)
    pallas_call x1, Pallas kernels, per_device(): pl.pallas_call(functools.partial(kernel, (snaps, nx, ny, nz), (gx_n, gy_n...  67 us
    unnamed x8, local copies, waits for them, and re-layouts  4.7 us

profile of v2, /device:TPU:0, one launch (start us, length us, event | category | flops | bytes accessed | tf_op | source)
XLA Modules:
  0.0 72.3 jit_solution(2036176778261518147)
XLA Ops:
  0.6 0.0 copy-start
  0.6 1.6 %copy-done = f32[128,8,4,128]{3,2,1,0:T(4,128)S(1)} copy-done((f32[128,8,4,128]{3,2,1,0:T(4,128)S(1)}, f32[128,8,4,128]{3,2,1,0:T(4,128)}, u32[]{:S(2)}) %copy-start) | copy-done | bytes 2097176
  2.2 0.0 copy-start.1
  2.2 0.8 %copy-done.1 = f32[3,8,4,128]{3,2,1,0:T(4,128)S(1)} copy-done((f32[3,8,4,128]{3,2,1,0:T(4,128)S(1)}, f32[3,8,4,128]{3,2,1,0:T(4,128)}, u32[]{:S(2)}) %copy-start.1) | copy-done | bytes 49176
  3.0 0.0 copy-start.2
  3.0 0.7 copy-done.2
  3.7 67.0 %pod.1 = (bf16[4096,128]{1,0:T(8,128)(2,1)S(1)}, f32[128,128]{1,0:T(8,128)S(1)}) custom-call(f32[4096,128]{1,0:T(8,128)S(1)} %bitcast.2, f32[8,4,128]{2,1,0:T(4,128)S(1)} %copy-done.2, f32[3,8,4,128]{3,2,1,0:T(4,128)S(1)} %copy-done.1), custom_call_target="tpu_custom_call" | custom-call | tf_op jit(solution)/shard_map/pod/pallas_call | solution.py:441
  70.7 1.0 %copy.7 = bf16[128,8,4,128]{3,2,1,0:T(4,128)(2,1)} copy(bf16[128,8,4,128]{3,2,1,0:T(4,128)(2,1)S(1)} %bitcast.3) | data formatting | bytes 2097152
  71.7 0.6 copy.8
Async XLA Ops:
  0.6 1.6 %copy-start = (f32[128,8,4,128]{3,2,1,0:T(4,128)S(1)}, f32[128,8,4,128]{3,2,1,0:T(4,128)}, u32[]{:S(2)}) copy-start(f32[128,8,4,128]{3,2,1,0:T(4,128)} %param.3) | copy-start | bytes 6291460
  2.2 0.8 %copy-start.1 = (f32[3,8,4,128]{3,2,1,0:T(4,128)S(1)}, f32[3,8,4,128]{3,2,1,0:T(4,128)}, u32[]{:S(2)}) copy-start(f32[3,8,4,128]{3,2,1,0:T(4,128)} %vel_ref.1) | copy-start | bytes 147460
  3.0 0.7 copy-start.2

commit v3 on v2

--- a/solution.py
+++ b/solution.py
@@ -26,8 +26,8 @@
 
 def kernel(
     dims, peers, chunk, cells_total,
-    snap_ref, visc_ref, vel_ref, modes_ref, factor_ref,
-    wide, passing, near_visc, pad_visc, coef, high, rest, rows_out, part_y, part_x, inv, low, diag,
+    snap_any, visc_any, vel_any, modes_ref, factor_ref,
+    snap_ref, visc_ref, vel_ref, load_snap, load_rest, wide, passing, near_visc, pad_visc, coef, high, rest, rows_out, part_y, part_x, inv, low, diag,
     send_halo, recv_halo, send_mid, recv_pass, send_pass, recv_mid, send_visc, recv_visc, send_y, recv_y, send_x, recv_x,
 ):
     snaps, nx, ny, nz = dims
@@ -41,6 +41,18 @@
 
     def along_x(other):
         return {"gx": other, "gy": gy}
+
+    def load(p):
+        here = pl.ds(p * chunk * cells, chunk * cells)
+        return pltpu.make_async_copy(snap_any.at[here], snap_ref.at[here], load_snap.at[p])
+
+    load_visc = pltpu.make_async_copy(visc_any, visc_ref, load_rest.at[0])
+    load_vel = pltpu.make_async_copy(vel_any, vel_ref, load_rest.at[1])
+    load(0).start()
+    load_visc.start()
+    for p in range(1, chunks):
+        load(p).start()
+    load_vel.start()
 
     barrier = pltpu.get_barrier_semaphore()
     for off in range(1, gy_n):
@@ -194,19 +206,23 @@
         for there, copy in copies:
             pl.when(there)(copy.wait_send)
 
+    load(0).wait()
     spread(0)
+    load_visc.wait()
     pl.semaphore_wait(barrier, gx_n + gy_n - 2)
-    start(visc_copies())
 
     def send_chunk(p):
         start_first(p)
         start(halo_copies(p))
 
     send_chunk(0)
+    start(visc_copies())
     for p in range(1, chunks):
+        load(p).wait()
         spread(p)
         if p == 1:
             send_chunk(1)
+    load_vel.wait()
 
     def border(way):
         rows_y = jnp.zeros((chunks, nx, 2, chunk, nz), jnp.float32)
@@ -352,19 +368,38 @@
             low[here, :] = jnp.zeros((chunk, snaps), jnp.float32)
         a = jnp.where(lane_s < chunk, g, jnp.where(lane_s == row_s + chunk, 1.0, 0.0))
         step = 8
-        for first in range(0, chunk, step):
-            columns = [jnp.broadcast_to(a[:, first + t:first + t + 1], a.shape) for t in range(step)]
-            rows = [a[first + t:first + t + 1, :] for t in range(step)]
+        a = a.reshape(chunk // step, step, snaps)
+        row_8 = lax.broadcasted_iota(jnp.int32, (step, snaps), 0)
+
+        def splat(x, row):
+            return jnp.broadcast_to(x[row:row + 1, :], (step, snaps))
+
+        done = []
+        for block in range(chunk // step):
+            first = block * step
+            own_rows, later = a[0], a[1:]
+            columns = [jnp.broadcast_to(later[:, :, first + t:first + t + 1], later.shape) for t in range(step)]
+            own_cols = [jnp.broadcast_to(own_rows[:, first + t:first + t + 1], (step, snaps)) for t in range(step)]
+            entries = {(t, u): splat(own_cols[t], u) for t in range(step) for u in range(t, step)}
+            rows = [splat(own_rows, t) for t in range(step)]
             for t in range(step):
-                k = first + t
-                col = columns[t]
-                over = 1.0 / col[k:k + 1, :]
+                over = 1.0 / entries[t, t]
                 scaled = rows[t] * over
-                a = a - jnp.where(row_s > k, col, 0.0) * scaled
+                if later.shape[0]:
+                    later = later - columns[t] * scaled[None]
                 for u in range(t + 1, step):
-                    entry = col[first + u:first + u + 1, :]
-                    columns[u] = columns[u] - col * (entry * over)
-                    rows[u] = rows[u] - entry * scaled
+                    ratio = entries[t, u] * over
+                    for v in range(u, step):
+                        entries[u, v] = entries[u, v] - ratio * entries[t, v]
+                    rows[u] = rows[u] - ratio * rows[t]
+                    if later.shape[0]:
+                        columns[u] = columns[u] - columns[t] * ratio[None]
+            kept = rows[0]
+            for t in range(1, step):
+                kept = jnp.where(row_8 == t, rows[t], kept)
+            done.append(kept)
+            a = later
+        a = jnp.concatenate(done, axis=0)
         pivots = jnp.sum(jnp.where(lane_s == row_s, a, 0.0), axis=1, keepdims=True)
         a = a / jnp.sqrt(pivots)
         upper = jnp.where((lane_s >= row_s) & (lane_s < chunk), a, 0.0)
@@ -446,9 +481,13 @@
             jax.ShapeDtypeStruct((snaps * cells, nz), jnp.bfloat16),
             jax.ShapeDtypeStruct((snaps, snaps), f32),
         ),
-        in_specs=[vmem] * 3,
+        in_specs=[pl.BlockSpec(memory_space=pl.ANY)] * 3,
         out_specs=(vmem, vmem),
         scratch_shapes=[
+            pltpu.VMEM((snaps * cells, nz), f32),
+            pltpu.VMEM((nx, ny, nz), f32),
+            pltpu.VMEM((3, nx, ny, nz), f32),
+            dma((chunks,)), dma((2,)),
             pltpu.VMEM((chunks, nx + 4, ny + 4, chunk, nz), f32),
             pltpu.VMEM((chunks, 2, nx // 2, 2, chunk, nz), f32),
             pltpu.VMEM((4, nx, ny, nz), f32),
@@ -467,7 +506,7 @@
             dma((chunks, gy_n)), dma((chunks, gy_n)), dma((chunks, gx_n)), dma((chunks, gx_n)),
         ],
         compiler_params=pltpu.CompilerParams(
-            collective_id=0, has_side_effects=True, vmem_limit_bytes=48 * 1024 * 1024
+            collective_id=0, has_side_effects=True, vmem_limit_bytes=60 * 1024 * 1024
         ),
         name="pod",
     )(snapshots.reshape(snaps * cells, nz), viscosity, velocity)

time: 72.6 us -> 72.3 us (level)
  local copies, waits for them, and re-layouts: 4.7 us -> 3.22 us
  Pallas kernels: 67 us -> 68.3 us
    unnamed x8 -> x4, local copies, waits for them, and re-layouts: 4.7 us -> 3.22 us
    pallas_call x1, Pallas kernels: 67 us -> 68.3 us  [per_device(): pl.pallas_call(functools.partial(kernel, (snaps, nx, ny, nz), (gx_n, gy_n...]
where the time goes in v3:
time: 72.3 us; the launch traced here: 72.1 us
  Pallas kernels  68.3 us (94%)
  local copies, waits for them, and re-layouts  3.22 us (4%)
    pallas_call x1, Pallas kernels, per_device(): pl.pallas_call(functools.partial(kernel, (snaps, nx, ny, nz), (gx_n, gy_n...  68.3 us
    unnamed x4, local copies, waits for them, and re-layouts  3.22 us

profile of v3, /device:TPU:0, one launch (start us, length us, event | category | flops | bytes accessed | tf_op | source)
XLA Modules:
  0.0 72.1 jit_solution(748428426572211997)
XLA Ops:
  0.6 68.3 %pod.1 = (bf16[4096,128]{1,0:T(8,128)(2,1)}, f32[128,128]{1,0:T(8,128)}) custom-call(f32[4096,128]{1,0:T(8,128)} %bitcast.2, f32[8,4,128]{2,1,0:T(4,128)} %visc_any.1, f32[3,8,4,128]{3,2,1,0:T(4,128)} %vel_any.1), custom_call_target="tpu_custom_call" | custom-call | tf_op jit(solution)/shard_map/pod/pallas_call | solution.py:476
  68.9 0.0 copy-start
  68.9 2.6 %copy.7 = bf16[128,8,4,128]{3,2,1,0:T(4,128)(2,1)} copy(bf16[128,8,4,128]{3,2,1,0:T(4,128)(2,1)} %bitcast.3) | data formatting | bytes 2097152
  71.5 0.0 copy-done
  71.5 0.6 copy.8
Async XLA Ops:
  68.9 2.6 %copy-start = (f32[128,128]{1,0:T(8,128)S(1)}, f32[128,128]{1,0:T(8,128)}, u32[]{:S(2)}) copy-start(f32[128,128]{1,0:T(8,128)} %get-tuple-element.9) | copy-start | bytes 196612

commit v4 on v3

--- a/solution.py
+++ b/solution.py
@@ -441,8 +441,6 @@
             send_chunk(p + 2)
         stencil(p)
         gram(p)
-        if p + 1 < chunks:
-            pass_on(p + 1, True)
         if p > 0:
             factor(p - 1)
         gram_x(p)
@@ -450,6 +448,8 @@
             pass_on(p + 2, False)
         if p > 0:
             modes(p - 1)
+        if p + 1 < chunks:
+            pass_on(p + 1, True)
     factor(chunks - 1)
     modes(chunks - 1)
     factor_ref[...] = low[...].T + diag[...]
@@ -481,7 +481,7 @@
             jax.ShapeDtypeStruct((snaps * cells, nz), jnp.bfloat16),
             jax.ShapeDtypeStruct((snaps, snaps), f32),
         ),
-        in_specs=[pl.BlockSpec(memory_space=pl.ANY)] * 3,
+        in_specs=[pl.BlockSpec(memory_space=pltpu.HBM)] * 3,
         out_specs=(vmem, vmem),
         scratch_shapes=[
             pltpu.VMEM((snaps * cells, nz), f32),
@@ -506,7 +506,7 @@
             dma((chunks, gy_n)), dma((chunks, gy_n)), dma((chunks, gx_n)), dma((chunks, gx_n)),
         ],
         compiler_params=pltpu.CompilerParams(
-            collective_id=0, has_side_effects=True, vmem_limit_bytes=60 * 1024 * 1024
+            collective_id=0, has_side_effects=True, vmem_limit_bytes=51 * 1024 * 1024
         ),
         name="pod",
     )(snapshots.reshape(snaps * cells, nz), viscosity, velocity)

time: 72.3 us -> 81.2 us (1.12)
  Pallas kernels: 68.3 us -> 77.2 us
    pallas_call x1, Pallas kernels: 68.3 us -> 77.2 us  [per_device(): pl.pallas_call(functools.partial(kernel, (snaps, nx, ny, nz), (gx_n, gy_n...]
    unnamed x4 -> x6, local copies, waits for them, and re-layouts: 3.22 us -> 3.11 us
where the time goes in v4:
time: 81.2 us; the launch traced here: 81 us
  Pallas kernels  77.2 us (95%)
  local copies, waits for them, and re-layouts  3.11 us (4%)
    pallas_call x1, Pallas kernels, per_device(): pl.pallas_call(functools.partial(kernel, (snaps, nx, ny, nz), (gx_n, gy_n...  77.2 us
    unnamed x6, local copies, waits for them, and re-layouts  3.11 us

profile of v4, /device:TPU:0, one launch (start us, length us, event | category | flops | bytes accessed | tf_op | source)
XLA Modules:
  0.0 81.0 jit_solution(1380840545277523221)
XLA Ops:
  0.6 0.0 copy-start
  0.6 0.8 copy-done
  1.4 0.0 copy-start.1
  1.4 0.7 copy-done.1
  2.1 77.2 %pod.1 = (bf16[4096,128]{1,0:T(8,128)(2,1)S(1)}, f32[128,128]{1,0:T(8,128)S(1)}) custom-call(f32[4096,128]{1,0:T(8,128)} %bitcast.3, f32[8,4,128]{2,1,0:T(4,128)S(1)} %copy-done.1, f32[3,8,4,128]{3,2,1,0:T(4,128)S(1)} %copy-done), custom_call_target="tpu_custom_call" | custom-call | tf_op jit(solution)/shard_map/pod/pallas_call | solution.py:476
  79.4 1.0 %copy.7 = bf16[128,8,4,128]{3,2,1,0:T(4,128)(2,1)} copy(bf16[128,8,4,128]{3,2,1,0:T(4,128)(2,1)S(1)} %bitcast.2) | data formatting | bytes 2097152
  80.4 0.6 copy.8
Async XLA Ops:
  0.6 0.8 copy-start
  1.4 0.7 copy-start.1

commit v5 on v4

--- a/solution.py
+++ b/solution.py
@@ -211,17 +211,14 @@
     load_visc.wait()
     pl.semaphore_wait(barrier, gx_n + gy_n - 2)
 
-    def send_chunk(p):
-        start_first(p)
-        start(halo_copies(p))
-
-    send_chunk(0)
     start(visc_copies())
+    start_first(0)
     for p in range(1, chunks):
         load(p).wait()
         spread(p)
-        if p == 1:
-            send_chunk(1)
+        if p < 3:
+            start_first(p)
+            start(halo_copies(p - 1))
     load_vel.wait()
 
     def border(way):
@@ -242,6 +239,8 @@
     inv[...] = jnp.zeros_like(inv)
     pad_visc[...] = jnp.zeros_like(pad_visc)
     pad_visc[1:nx + 1, 1:ny + 1, :] = visc_ref[...]
+    pass_on(0, False)
+    pass_on(0, True)
     wait_recv(visc_copies(), arrives)
 
     def visc_border(way):
@@ -430,26 +429,25 @@
 
     for p in range(chunks):
         if p == 0:
-            pass_on(0, False)
-            pass_on(0, True)
             pass_on(1, False)
+            pass_on(1, True)
         wait_recv(halo_copies(p), arrives_direct)
         wait_mid(p)
         if p + 2 < chunks:
+            if p + 3 < chunks:
+                start_first(p + 3)
             wait_send(halo_copies(p))
-            wait_mid_sent(p)
-            send_chunk(p + 2)
+            start(halo_copies(p + 2))
         stencil(p)
         gram(p)
+        if p + 2 < chunks:
+            pass_on(p + 2, False)
+            pass_on(p + 2, True)
         if p > 0:
             factor(p - 1)
         gram_x(p)
-        if p + 2 < chunks:
-            pass_on(p + 2, False)
         if p > 0:
             modes(p - 1)
-        if p + 1 < chunks:
-            pass_on(p + 1, True)
     factor(chunks - 1)
     modes(chunks - 1)
     factor_ref[...] = low[...].T + diag[...]
@@ -458,7 +456,7 @@
     for p in range(chunks):
         if p + 2 >= chunks:
             wait_send(halo_copies(p))
-            wait_mid_sent(p)
+        wait_mid_sent(p)
         wait_passed(p)
         for axis in ("gy", "gx"):
             for copy in sum_copies(p, axis)[0]:

time: 81.2 us -> 72.3 us (0.89)
  Pallas kernels: 77.2 us -> 68.3 us
    pallas_call x1, Pallas kernels: 77.2 us -> 68.3 us  [per_device(): pl.pallas_call(functools.partial(kernel, (snaps, nx, ny, nz), (gx_n, gy_n...]
where the time goes in v5:
time: 72.3 us; the launch traced here: 72.1 us
  Pallas kernels  68.3 us (94%)
  local copies, waits for them, and re-layouts  3.11 us (4%)
    pallas_call x1, Pallas kernels, per_device(): pl.pallas_call(functools.partial(kernel, (snaps, nx, ny, nz), (gx_n, gy_n...  68.3 us
    unnamed x6, local copies, waits for them, and re-layouts  3.11 us

profile of v5, /device:TPU:0, one launch (start us, length us, event | category | flops | bytes accessed | tf_op | source)
XLA Modules:
  0.0 72.1 jit_solution(4540376910454095985)
XLA Ops:
  0.6 0.0 copy-start
  0.6 0.8 %copy-done = f32[3,8,4,128]{3,2,1,0:T(4,128)S(1)} copy-done((f32[3,8,4,128]{3,2,1,0:T(4,128)S(1)}, f32[3,8,4,128]{3,2,1,0:T(4,128)}, u32[]{:S(2)}) %copy-start) | copy-done | bytes 49176
  1.4 0.0 copy-start.1
  1.4 0.7 copy-done.1
  2.1 68.3 %pod.1 = (bf16[4096,128]{1,0:T(8,128)(2,1)S(1)}, f32[128,128]{1,0:T(8,128)S(1)}) custom-call(f32[4096,128]{1,0:T(8,128)} %bitcast.3, f32[8,4,128]{2,1,0:T(4,128)S(1)} %copy-done.1, f32[3,8,4,128]{3,2,1,0:T(4,128)S(1)} %copy-done), custom_call_target="tpu_custom_call" | custom-call | tf_op jit(solution)/shard_map/pod/pallas_call | solution.py:474
  70.5 1.0 %copy.7 = bf16[128,8,4,128]{3,2,1,0:T(4,128)(2,1)} copy(bf16[128,8,4,128]{3,2,1,0:T(4,128)(2,1)S(1)} %bitcast.2) | data formatting | bytes 2097152
  71.4 0.6 copy.8
Async XLA Ops:
  0.6 0.8 %copy-start = (f32[3,8,4,128]{3,2,1,0:T(4,128)S(1)}, f32[3,8,4,128]{3,2,1,0:T(4,128)}, u32[]{:S(2)}) copy-start(f32[3,8,4,128]{3,2,1,0:T(4,128)} %vel_any.1) | copy-start | bytes 147460
  1.4 0.7 copy-start.1

commit v6 on v5

--- a/solution.py
+++ b/solution.py
@@ -216,9 +216,9 @@
     for p in range(1, chunks):
         load(p).wait()
         spread(p)
-        if p < 3:
-            start_first(p)
-            start(halo_copies(p - 1))
+        if p == 1:
+            start(halo_copies(0))
+            start_first(1)
     load_vel.wait()
 
     def border(way):
@@ -428,21 +428,18 @@
         modes_ref[p * chunk * cells:top * cells, :] = rows_out[...].astype(jnp.bfloat16)
 
     for p in range(chunks):
-        if p == 0:
-            pass_on(1, False)
-            pass_on(1, True)
+        wait_send(halo_copies(p))
+        if p + 1 < chunks:
+            start(halo_copies(p + 1))
+        if p + 2 < chunks:
+            start_first(p + 2)
+        if p + 1 < chunks:
+            pass_on(p + 1, False)
+            pass_on(p + 1, True)
         wait_recv(halo_copies(p), arrives_direct)
         wait_mid(p)
-        if p + 2 < chunks:
-            if p + 3 < chunks:
-                start_first(p + 3)
-            wait_send(halo_copies(p))
-            start(halo_copies(p + 2))
         stencil(p)
         gram(p)
-        if p + 2 < chunks:
-            pass_on(p + 2, False)
-            pass_on(p + 2, True)
         if p > 0:
             factor(p - 1)
         gram_x(p)
@@ -454,8 +451,6 @@
 
     wait_send(visc_copies())
     for p in range(chunks):
-        if p + 2 >= chunks:
-            wait_send(halo_copies(p))
         wait_mid_sent(p)
         wait_passed(p)
         for axis in ("gy", "gx"):

time: 72.3 us -> 70.6 us (0.976)
  Pallas kernels: 68.3 us -> 66.6 us
    pallas_call x1, Pallas kernels: 68.3 us -> 66.6 us  [per_device(): pl.pallas_call(functools.partial(kernel, (snaps, nx, ny, nz), (gx_n, gy_n...]
where the time goes in v6:
time: 70.6 us; the launch traced here: 70.3 us
  Pallas kernels  66.6 us (94%)
  local copies, waits for them, and re-layouts  3.11 us (4%)
    pallas_call x1, Pallas kernels, per_device(): pl.pallas_call(functools.partial(kernel, (snaps, nx, ny, nz), (gx_n, gy_n...  66.6 us
    unnamed x6, local copies, waits for them, and re-layouts  3.11 us

profile of v6, /device:TPU:0, one launch (start us, length us, event | category | flops | bytes accessed | tf_op | source)
XLA Modules:
  0.0 70.3 jit_solution(12004561179455114999)
XLA Ops:
  0.6 0.0 copy-start
  0.6 0.8 %copy-done = f32[3,8,4,128]{3,2,1,0:T(4,128)S(1)} copy-done((f32[3,8,4,128]{3,2,1,0:T(4,128)S(1)}, f32[3,8,4,128]{3,2,1,0:T(4,128)}, u32[]{:S(2)}) %copy-start) | copy-done | bytes 49176
  1.4 0.0 copy-start.1
  1.4 0.7 %copy-done.1 = f32[8,4,128]{2,1,0:T(4,128)S(1)} copy-done((f32[8,4,128]{2,1,0:T(4,128)S(1)}, f32[8,4,128]{2,1,0:T(4,128)}, u32[]{:S(2)}) %copy-start.1) | copy-done | bytes 16408
  2.1 66.6 %pod.1 = (bf16[4096,128]{1,0:T(8,128)(2,1)S(1)}, f32[128,128]{1,0:T(8,128)S(1)}) custom-call(f32[4096,128]{1,0:T(8,128)} %bitcast.3, f32[8,4,128]{2,1,0:T(4,128)S(1)} %copy-done.1, f32[3,8,4,128]{3,2,1,0:T(4,128)S(1)} %copy-done), custom_call_target="tpu_custom_call" | custom-call | tf_op jit(solution)/shard_map/pod/pallas_call | solution.py:469
  68.7 1.0 %copy.7 = bf16[128,8,4,128]{3,2,1,0:T(4,128)(2,1)} copy(bf16[128,8,4,128]{3,2,1,0:T(4,128)(2,1)S(1)} %bitcast.2) | data formatting | bytes 2097152
  69.7 0.6 copy.8
Async XLA Ops:
  0.6 0.8 %copy-start = (f32[3,8,4,128]{3,2,1,0:T(4,128)S(1)}, f32[3,8,4,128]{3,2,1,0:T(4,128)}, u32[]{:S(2)}) copy-start(f32[3,8,4,128]{3,2,1,0:T(4,128)} %vel_any.1) | copy-start | bytes 147460
  1.4 0.7 %copy-start.1 = (f32[8,4,128]{2,1,0:T(4,128)S(1)}, f32[8,4,128]{2,1,0:T(4,128)}, u32[]{:S(2)}) copy-start(f32[8,4,128]{2,1,0:T(4,128)} %visc_any.1) | copy-start | bytes 49156

commit v7 on v5

--- a/solution.py
+++ b/solution.py
@@ -217,8 +217,8 @@
         load(p).wait()
         spread(p)
         if p < 3:
+            start(halo_copies(p - 1))
             start_first(p)
-            start(halo_copies(p - 1))
     load_vel.wait()
 
     def border(way):
@@ -431,18 +431,18 @@
         if p == 0:
             pass_on(1, False)
             pass_on(1, True)
-        wait_recv(halo_copies(p), arrives_direct)
-        wait_mid(p)
+        wait_send(halo_copies(p))
         if p + 2 < chunks:
-            if p + 3 < chunks:
-                start_first(p + 3)
-            wait_send(halo_copies(p))
             start(halo_copies(p + 2))
-        stencil(p)
-        gram(p)
+        if p + 3 < chunks:
+            start_first(p + 3)
         if p + 2 < chunks:
             pass_on(p + 2, False)
             pass_on(p + 2, True)
+        wait_recv(halo_copies(p), arrives_direct)
+        wait_mid(p)
+        stencil(p)
+        gram(p)
         if p > 0:
             factor(p - 1)
         gram_x(p)
@@ -454,8 +454,6 @@
 
     wait_send(visc_copies())
     for p in range(chunks):
-        if p + 2 >= chunks:
-            wait_send(halo_copies(p))
         wait_mid_sent(p)
         wait_passed(p)
         for axis in ("gy", "gx"):
@@ -466,7 +464,7 @@
 def per_device(gx_n, gy_n, snapshots, viscosity, velocity):
     snaps, nx, ny, nz = snapshots.shape
     cells = nx * ny
-    chunk = snaps // 4
+    chunk = snaps // 8
     chunks = snaps // chunk
     f32 = jnp.float32
     dma = pltpu.SemaphoreType.DMA

time: 72.3 us -> 81.8 us (1.13)
  Pallas kernels: 68.3 us -> 77.8 us
    pallas_call x1, Pallas kernels: 68.3 us -> 77.8 us  [per_device(): pl.pallas_call(functools.partial(kernel, (snaps, nx, ny, nz), (gx_n, gy_n...]
where the time goes in v7:
time: 81.8 us; the launch traced here: 81.6 us
  Pallas kernels  77.8 us (95%)
  local copies, waits for them, and re-layouts  3.11 us (4%)
    pallas_call x1, Pallas kernels, per_device(): pl.pallas_call(functools.partial(kernel, (snaps, nx, ny, nz), (gx_n, gy_n...  77.8 us
    unnamed x6, local copies, waits for them, and re-layouts  3.11 us

profile of v7, /device:TPU:0, one launch (start us, length us, event | category | flops | bytes accessed | tf_op | source)
XLA Modules:
  0.0 81.6 jit_solution(3564513013544549515)
XLA Ops:
  0.6 0.0 copy-start
  0.6 0.8 copy-done
  1.4 0.0 copy-start.1
  1.4 0.7 copy-done.1
  2.1 77.8 %pod.1 = (bf16[4096,128]{1,0:T(8,128)(2,1)S(1)}, f32[128,128]{1,0:T(8,128)S(1)}) custom-call(f32[4096,128]{1,0:T(8,128)} %bitcast.3, f32[8,4,128]{2,1,0:T(4,128)S(1)} %copy-done.1, f32[3,8,4,128]{3,2,1,0:T(4,128)S(1)} %copy-done), custom_call_target="tpu_custom_call" | custom-call | tf_op jit(solution)/shard_map/pod/pallas_call | solution.py:472
  80.0 1.0 %copy.7 = bf16[128,8,4,128]{3,2,1,0:T(4,128)(2,1)} copy(bf16[128,8,4,128]{3,2,1,0:T(4,128)(2,1)S(1)} %bitcast.2) | data formatting | bytes 2097152
  81.0 0.6 copy.8
Async XLA Ops:
  0.6 0.8 copy-start
  1.4 0.7 copy-start.1

commit v8 on v6

--- a/solution.py
+++ b/solution.py
@@ -213,11 +213,11 @@
 
     start(visc_copies())
     start_first(0)
+    start(halo_copies(0))
     for p in range(1, chunks):
         load(p).wait()
         spread(p)
         if p == 1:
-            start(halo_copies(0))
             start_first(1)
     load_vel.wait()
 
@@ -440,13 +440,9 @@
         wait_mid(p)
         stencil(p)
         gram(p)
-        if p > 0:
-            factor(p - 1)
         gram_x(p)
-        if p > 0:
-            modes(p - 1)
-    factor(chunks - 1)
-    modes(chunks - 1)
+        factor(p)
+        modes(p)
     factor_ref[...] = low[...].T + diag[...]
 
     wait_send(visc_copies())
@@ -461,7 +457,7 @@
 def per_device(gx_n, gy_n, snapshots, viscosity, velocity):
     snaps, nx, ny, nz = snapshots.shape
     cells = nx * ny
-    chunk = snaps // 4
+    chunk = snaps // 2
     chunks = snaps // chunk
     f32 = jnp.float32
     dma = pltpu.SemaphoreType.DMA

time: 70.6 us -> 75.1 us (1.064)
  Pallas kernels: 66.6 us -> 71 us
    pallas_call x1, Pallas kernels: 66.6 us -> 71 us  [per_device(): pl.pallas_call(functools.partial(kernel, (snaps, nx, ny, nz), (gx_n, gy_n...]
where the time goes in v8:
time: 75.1 us; the launch traced here: 74.8 us
  Pallas kernels  71 us (95%)
  local copies, waits for them, and re-layouts  3.11 us (4%)
    pallas_call x1, Pallas kernels, per_device(): pl.pallas_call(functools.partial(kernel, (snaps, nx, ny, nz), (gx_n, gy_n...  71 us
    unnamed x6, local copies, waits for them, and re-layouts  3.11 us

profile of v8, /device:TPU:0, one launch (start us, length us, event | category | flops | bytes accessed | tf_op | source)
XLA Modules:
  0.0 74.8 jit_solution(17354161311222025713)
XLA Ops:
  0.6 0.0 copy-start
  0.6 0.8 %copy-done = f32[3,8,4,128]{3,2,1,0:T(4,128)S(1)} copy-done((f32[3,8,4,128]{3,2,1,0:T(4,128)S(1)}, f32[3,8,4,128]{3,2,1,0:T(4,128)}, u32[]{:S(2)}) %copy-start) | copy-done | bytes 49176
  1.4 0.0 copy-start.1
  1.4 0.7 copy-done.1
  2.1 71.0 %pod.1 = (bf16[4096,128]{1,0:T(8,128)(2,1)S(1)}, f32[128,128]{1,0:T(8,128)S(1)}) custom-call(f32[4096,128]{1,0:T(8,128)} %bitcast.3, f32[8,4,128]{2,1,0:T(4,128)S(1)} %copy-done.1, f32[3,8,4,128]{3,2,1,0:T(4,128)S(1)} %copy-done), custom_call_target="tpu_custom_call" | custom-call | tf_op jit(solution)/shard_map/pod/pallas_call | solution.py:465
  73.2 1.0 %copy.7 = bf16[128,8,4,128]{3,2,1,0:T(4,128)(2,1)} copy(bf16[128,8,4,128]{3,2,1,0:T(4,128)(2,1)S(1)} %bitcast.2) | data formatting | bytes 2097152
  74.2 0.6 copy.8
Async XLA Ops:
  0.6 0.8 %copy-start = (f32[3,8,4,128]{3,2,1,0:T(4,128)S(1)}, f32[3,8,4,128]{3,2,1,0:T(4,128)}, u32[]{:S(2)}) copy-start(f32[3,8,4,128]{3,2,1,0:T(4,128)} %vel_any.1) | copy-start | bytes 147460
  1.4 0.7 copy-start.1
